TPU v7x, 32 devices: a whole 2x2x4 slice. The times are simulated.
32 devices in a mesh: space: 8 (over z, x), member: 4 (over y, core).
Axes of the slice: x: 2, y: 2, z: 4, core: 2. Of those that a mesh axis runs over, the one named last changes fastest.
Arguments:
- fields: float32 [8, 16, 128, 256], P('member', 'space'), may hold values from -6 to 6
- velocity: float32 [16, 128, 256], P('space'), may hold values from 0.2 to 0.6
- building: int32 [16, 128, 256], P('space'), may hold values 0 or 1
- inflow_table: float32 [32, 128, 256], replicated, may hold values from -6 to 6
- inflow_index: int32 [8], P('member'), may hold values from 0 to 31
Outputs:
- fields_now: float32 [8, 16, 128, 256], P('member', 'space')
- r_factor: float32 [8, 8], replicated
All inputs are finite; a program needn't handle non-finite values. No bound on the sum of `building` on one device may be relied on, other than what follows from the above.
Results may differ from a plain program's by a relative error of at most 0.0003.
Values may be sent and summed in bfloat16 or wider, within the bound.
A program may use at most 64 MiB of HBM per device.

v0:
```python
import jax
import jax.numpy as jnp
from jax import lax
from jax.sharding import PartitionSpec as P

STEPS = 2
kappa_rate = 0.05
shrink_weight = 0.1
contract_dims = (((1,), (1,)), ((), ()))


def extended_2(block, sides, width):
    for axis, dim in sides:
        count = lax.axis_size(axis)
        forward = [(i, i + 1) for i in range(count - 1)]
        backward = [(target, source) for source, target in forward]
        low = lax.ppermute(
            lax.slice_in_dim(block, block.shape[dim] - width, None, axis=dim), axis, forward
        )
        high = lax.ppermute(lax.slice_in_dim(block, 0, width, axis=dim), axis, backward)
        block = jnp.concatenate([low, block, high], axis=dim)
    return block


def from_behind(block, axis, distance):
    devices = range(lax.axis_size(axis))
    route = [((i - distance) % len(devices), i) for i in devices]
    return lax.ppermute(block, axis, route)


def advance(extended, fluid_cells, courant):
    upwind = extended[:, :-2]
    centre = extended[:, 1:-1]
    downwind = extended[:, 2:]
    in_plane = (
        jnp.roll(centre, 1, 2)
        + jnp.roll(centre, -1, 2)
        + jnp.roll(centre, 1, 3)
        + jnp.roll(centre, -1, 3)
    )
    return fluid_cells * (
        centre
        + courant * (upwind - centre)
        + kappa_rate * (upwind + downwind + in_plane - 6.0 * centre)
    )


def local(fields, velocity, building, inflow_table, inflow_index):
    mem_dev = fields.shape[0]
    slab_depth = fields.shape[1]
    plane_rows = fields.shape[2]
    plane_cols = fields.shape[3]
    patterns = inflow_table.shape[0]
    fluid_cells = (1 - building).astype(jnp.float32)
    pattern_pick = (inflow_index[:, None] == jnp.arange(patterns, dtype=jnp.int32)[None, :]).astype(
        jnp.float32
    )
    inflow_plane = jnp.dot(
        pattern_pick,
        inflow_table.reshape(patterns, plane_rows * plane_cols),
        precision=lax.Precision.HIGHEST,
        preferred_element_type=jnp.float32,
    ).reshape(mem_dev, plane_rows, plane_cols)
    at_inflow = lax.axis_index("space") == 0
    fields_now = fields
    for sweep_index in range(STEPS):
        extended = extended_2(fields_now, (("space", 1),), 1)
        extended = extended.at[:, 0].set(jnp.where(at_inflow, inflow_plane, extended[:, 0]))
        fields_now = advance(extended, fluid_cells, velocity)
    groups = lax.axis_size("member")
    all_members = mem_dev * groups
    member_sum = jnp.sum(fields_now, 0)
    ensemble_mean = (
        lax.psum(member_sum.astype(jnp.bfloat16), "member").astype(jnp.float32) / all_members
    )
    anomaly = (
        (fields_now - ensemble_mean)
        .astype(jnp.bfloat16)
        .reshape(mem_dev, slab_depth * plane_rows * plane_cols)
    )
    my_group = lax.axis_index("member")
    cells_all = slab_depth * lax.axis_size("space") * plane_rows * plane_cols
    empty_rows = jnp.zeros((mem_dev, all_members), jnp.float32)

    def place(gram_tile, panel_piece, first_row):
        gram_block = lax.dot_general(
            anomaly, panel_piece, contract_dims, preferred_element_type=jnp.float32
        )
        return lax.dynamic_update_slice(
            gram_tile, gram_block, (jnp.int32(0), jnp.asarray(first_row))
        )

    gram_tile = place(empty_rows, anomaly, my_group * mem_dev)

    def turn(sweep_index, loop_state):
        tile_now, panel_held = loop_state
        panel_held = from_behind(panel_held, "member", 1)
        source = (my_group - sweep_index) % groups
        return (place(tile_now, panel_held, source * mem_dev), panel_held)

    gram_tile, panel_held = lax.fori_loop(1, groups, turn, (gram_tile, anomaly))
    gram_tile = gram_tile / cells_all
    summed = lax.psum(gram_tile, "space")
    gram_full = lax.all_gather(summed, "member", axis=0, tiled=True)
    r_factor = jnp.linalg.cholesky(
        gram_full + shrink_weight * jnp.eye(all_members, dtype=jnp.float32)
    ).T
    return (fields_now, r_factor)


def solution(mesh):
    placed = (
        P("member", "space", None, None),
        P("space", None, None),
        P("space", None, None),
        P(),
        P("member"),
    )
    return jax.shard_map(
        local,
        mesh=mesh,
        in_specs=placed,
        out_specs=(P("member", "space", None, None), P()),
        check_vma=False,
    )
```

profile of v0, /device:TPU:0, one launch (start us, length us, event | category | flops | bytes accessed | tf_op | source)
XLA Modules:
  0.0 151.2 jit_solution(6526579312249673913)
XLA Ops:
  7.2 1.4 copy.24
  8.9 4.9 %collective-permute-start.1 = (f32[2,1,128,256]{3,0,2,1:T(2,128)S(1)}, f32[2,1,128,256]{3,0,2,1:T(2,128)S(1)}, u32[]{:S(2)}, u32[]{:S(2)}) collective-permute-start(f32[2,1,128,256]{3,0,2,1:T(2,128)S(1)} %get-tuple-element.196), channel_id=1, source_target_pairs={{0,4},{4,8},{8,12},{12,16},{16,20},{20,24},{24,28},{1,5},{5,9},{9,... | collective-permute-start | bytes 786440 | tf_op jit(solution)/shard_map/ppermute | solution.py:17
  13.7 1.3 collective-permute-start.2
  15.0 1.0 subtract_convert_fusion.1
  16.0 8.9 %collective-permute-done.1 = f32[2,1,128,256]{3,0,2,1:T(2,128)S(1)} collective-permute-done((f32[2,1,128,256]{3,0,2,1:T(2,128)S(1)}, f32[2,1,128,256]{3,0,2,1:T(2,128)S(1)}, u32[]{:S(2)}, u32[]{:S(2)}) %collective-permute-start.1) | collective-permute-done | bytes 262176 | tf_op jit(solution)/shard_map/ppermute | solution.py:17
  25.4 6.0 %bitcast_dynamic-update-slice_fusion.1 = (f32[2,4,128,256]{3,0,2,1:T(2,128)S(1)}, f32[2,128,256]{2,0,1:T(2,128)S(1)}) fusion(f32[2,4,128,256]{3,0,2,1:T(2,128)S(1)} %pad_maximum_fusion, f32[2,1,128,256]{3,0,2,1:T(2,128)S(1)} %collective-permute-done.1, pred[]{:T(512)S(6)} %eq.25, s32[2]{0:T(128)S(1)} %copy-done.1, f32[4,8,128,256]{3,2,1,0:T(8,128)} %bitcast.51), kind=kOutput, calls=%fused_computation.27 | convolution fusion | flops 25231424 | bytes 4981249 | tf_op jit(solution)/shard_map/dot_general | solution.py:58
  32.7 1.9 %fusion.15 = f32[2,2,128,256]{3,0,2,1:T(2,128)S(1)} fusion(f32[2,2,128,1]{3,0,2,1:T(2,128)S(1)} %get-tuple-element.191, f32[2,2,128,255]{3,0,2,1:T(2,128)S(1)} %get-tuple-element.193, f32[2,2,128,255]{3,0,2,1:T(2,128)S(1)} %get-tuple-element.192, f32[2,2,128,1]{3,0,2,1:T(2,128)S(1)} %get-tuple-element.190, f32[2,2,1,256]{3,0,2,1:T(2,128)S(1)} %get-tuple-element.187, ...), kind=kLoop, calls=%fused_computation.23 | loop fusion | flops 2228224 | bytes 4718592 | tf_op jit(solution)/shard_map/mul | solution.py:41
  34.8 4.4 %collective-permute-start.3 = (f32[2,1,128,256]{3,0,2,1:T(2,128)S(1)}, f32[2,1,128,256]{3,0,2,1:T(2,128)S(1)}, u32[]{:S(2)}, u32[]{:S(2)}) collective-permute-start(f32[2,1,128,256]{3,0,2,1:T(2,128)S(1)} %get-tuple-element.194), channel_id=1, source_target_pairs={{0,4},{4,8},{8,12},{12,16},{16,20},{20,24},{24,28},{1,5},{5,9},{9,... | collective-permute-start | bytes 786440 | tf_op jit(solution)/shard_map/ppermute | solution.py:17
  39.3 1.5 collective-permute-start.4
  40.7 3.2 %collective-permute-done.3 = f32[2,1,128,256]{3,0,2,1:T(2,128)S(1)} collective-permute-done((f32[2,1,128,256]{3,0,2,1:T(2,128)S(1)}, f32[2,1,128,256]{3,0,2,1:T(2,128)S(1)}, u32[]{:S(2)}, u32[]{:S(2)}) %collective-permute-start.3) | collective-permute-done | bytes 262176 | tf_op jit(solution)/shard_map/ppermute | solution.py:17
  43.9 5.9 %collective-permute-done.4 = f32[2,1,128,256]{3,0,2,1:T(2,128)S(1)} collective-permute-done((f32[2,1,128,256]{3,0,2,1:T(2,128)S(1)}, f32[2,1,128,256]{3,0,2,1:T(2,128)S(1)}, u32[]{:S(2)}, u32[]{:S(2)}) %collective-permute-start.4) | collective-permute-done | bytes 262176 | tf_op jit(solution)/shard_map/ppermute | solution.py:20
  51.8 3.2 %fusion.22 = (bf16[2,128,256]{2,1,0:T(8,128)(2,1)}, f32[2,2,128,256]{3,0,2,1:T(2,128)S(1)}) fusion(f32[2,2,128,1]{3,0,2,1:T(2,128)S(1)} %get-tuple-element.183, f32[2,2,128,255]{3,0,2,1:T(2,128)S(1)} %get-tuple-element.185, f32[2,2,128,255]{3,0,2,1:T(2,128)S(1)} %get-tuple-element.184, f32[2,2,128,1]{3,0,2,1:T(2,128)S(1)} %get-tuple-element.182, ...), kind=kLoop, calls=%fused_computation.44 | loop fusion | flops 2293760 | bytes 4849664 | tf_op jit(solution)/shard_map/reduce_sum | solution.py:72
  55.0 35.5 %all-reduce.2.cloned.1.call-done = bf16[2,128,256]{2,1,0:T(8,128)(2,1)} async-done(((bf16[2,128,256]{2,1,0:T(8,128)(2,1)}), bf16[2,128,256]{2,1,0:T(8,128)(2,1)}) %all-reduce.2.cloned.1.call-update) | async-done | bytes 131088 | tf_op jit(solution)/shard_map/psum | solution.py:74
  90.5 0.9 convert_multiply_fusion
  91.7 0.9 convolution_bitcast_fusion
  92.9 21.1 %while.19 = (s32[]{:T(128)}, f32[2,8]{1,0:T(2,128)S(1)}, bf16[2,65536]{1,0:T(2,128)(2,1)S(1)}, bf16[2,65536]{1,0:T(2,128)(2,1)S(1)}, s32[]{:T(128)}, /*index=5*/...) while((s32[]{:T(128)}, f32[2,8]{1,0:T(2,128)S(1)}, ...), condition=%wide.region_3.4_spmd, body=%wide.region_2.3_spmd.sunk | while | flops 524306 | bytes 2097520 | solution.py:101
  93.0 5.8 %collective-permute-done = bf16[2,65536]{1,0:T(2,128)(2,1)S(1)} collective-permute-done((bf16[2,65536]{1,0:T(2,128)(2,1)S(1)}, bf16[2,65536]{1,0:T(2,128)(2,1)S(1)}, u32[]{:S(2)}, u32[]{:S(2)}) %collective-permute-start) | collective-permute-done | bytes 262176 | tf_op jit(solution)/shard_map/while/body/eval_jaxpr/ppermute | solution.py:28
  98.8 0.8 fusion.44
  100.0 5.8 %collective-permute-done = bf16[2,65536]{1,0:T(2,128)(2,1)S(1)} collective-permute-done((bf16[2,65536]{1,0:T(2,128)(2,1)S(1)}, bf16[2,65536]{1,0:T(2,128)(2,1)S(1)}, u32[]{:S(2)}, u32[]{:S(2)}) %collective-permute-start) | collective-permute-done | bytes 262176 | tf_op jit(solution)/shard_map/while/body/eval_jaxpr/ppermute | solution.py:28
  107.1 5.8 %collective-permute-done = bf16[2,65536]{1,0:T(2,128)(2,1)S(1)} collective-permute-done((bf16[2,65536]{1,0:T(2,128)(2,1)S(1)}, bf16[2,65536]{1,0:T(2,128)(2,1)S(1)}, u32[]{:S(2)}, u32[]{:S(2)}) %collective-permute-start) | collective-permute-done | bytes 262176 | tf_op jit(solution)/shard_map/while/body/eval_jaxpr/ppermute | solution.py:28
  114.0 0.8 copy.32
  114.9 21.3 %psum.15 = f32[2,8]{1,0:T(2,128)S(1)} all-reduce(f32[2,8]{1,0:T(2,128)S(1)} %broadcast_multiply_fusion), channel_id=1, replica_groups=mesh['space'=8,'member'=4] {'space'}, use_global_device_ids=true, to_apply=%region_4.5 | all-reduce | flops 16 | bytes 128 | tf_op jit(solution)/shard_map/psum | solution.py:103
  136.2 5.1 %all-gather = f32[4,2,8]{2,1,0:T(2,128)S(1)} all-gather(f32[1,2,8]{2,1,0:T(2,128)S(1)} %bitcast.55), channel_id=1, replica_groups=mesh['space'=8,'member'=4] {'member'}, dimensions={0}, use_global_device_ids=true | all-gather | bytes 320 | tf_op jit(solution)/shard_map/all_gather | solution.py:104
  143.1 1.3 select_bitcast_fusion
  (44 shorter events, 9.5 us)
Async XLA Ops:
  7.2 18.2 %copy-start.1 = (s32[2]{0:T(128)S(1)}, s32[2]{0:T(128)}, u32[]{:S(2)}) copy-start(s32[2]{0:T(128)} %param.15) | copy-start | bytes 28
  7.2 83.3 %all-reduce.2.cloned.1.call-start = ((), (), s32[]{:S(2)}) async-start(), calls=%async_computation | async-start | bytes 262144 | tf_op jit(solution)/shard_map/psum | solution.py:74
  8.9 16.0 %collective-permute-start.1 = (f32[2,1,128,256]{3,0,2,1:T(2,128)S(1)}, f32[2,1,128,256]{3,0,2,1:T(2,128)S(1)}, u32[]{:S(2)}, u32[]{:S(2)}) collective-permute-start(f32[2,1,128,256]{3,0,2,1:T(2,128)S(1)} %get-tuple-element.196), channel_id=1, source_target_pairs={{0,4},{4,8},{8,12},{12,16},{16,20},{20,24},{24,28},{1,5},{5,9},{9,... | collective-permute-start | bytes 786440 | tf_op jit(solution)/shard_map/ppermute | solution.py:17
  13.7 11.2 %collective-permute-start.2 = (f32[2,1,128,256]{3,0,2,1:T(2,128)S(1)}, f32[2,1,128,256]{3,0,2,1:T(2,128)S(1)}, u32[]{:S(2)}, u32[]{:S(2)}) collective-permute-start(f32[2,1,128,256]{3,0,2,1:T(2,128)S(1)} %get-tuple-element.197), channel_id=1, source_target_pairs={{4,0},{8,4},{12,8},{16,12},{20,16},{24,20},{28,24},{5,1},{9,5},{13... | collective-permute-start | bytes 786440 | tf_op jit(solution)/shard_map/ppermute | solution.py:20
  25.4 7.3 %copy-start = (f32[2,128,256]{2,1,0:T(8,128)S(1)}, f32[2,128,256]{2,1,0:T(8,128)}, u32[]{:S(2)}) copy-start(f32[2,128,256]{2,1,0:T(8,128)} %param.12) | copy-start | bytes 786436
  34.8 9.1 %collective-permute-start.3 = (f32[2,1,128,256]{3,0,2,1:T(2,128)S(1)}, f32[2,1,128,256]{3,0,2,1:T(2,128)S(1)}, u32[]{:S(2)}, u32[]{:S(2)}) collective-permute-start(f32[2,1,128,256]{3,0,2,1:T(2,128)S(1)} %get-tuple-element.194), channel_id=1, source_target_pairs={{0,4},{4,8},{8,12},{12,16},{16,20},{20,24},{24,28},{1,5},{5,9},{9,... | collective-permute-start | bytes 786440 | tf_op jit(solution)/shard_map/ppermute | solution.py:17
  39.3 10.5 %collective-permute-start.4 = (f32[2,1,128,256]{3,0,2,1:T(2,128)S(1)}, f32[2,1,128,256]{3,0,2,1:T(2,128)S(1)}, u32[]{:S(2)}, u32[]{:S(2)}) collective-permute-start(f32[2,1,128,256]{3,0,2,1:T(2,128)S(1)} %get-tuple-element.195), channel_id=1, source_target_pairs={{4,0},{8,4},{12,8},{16,12},{20,16},{24,20},{28,24},{5,1},{9,5},{13... | collective-permute-start | bytes 786440 | tf_op jit(solution)/shard_map/ppermute | solution.py:20
  92.9 5.8 %collective-permute-start = (bf16[2,65536]{1,0:T(2,128)(2,1)S(1)}, bf16[2,65536]{1,0:T(2,128)(2,1)S(1)}, u32[]{:S(2)}, u32[]{:S(2)}) collective-permute-start(bf16[2,65536]{1,0:T(2,128)(2,1)S(1)} %get-tuple-element.244), channel_id=1, source_target_pairs={{3,0},{0,1},{1,2},{2,3},{7,4},{4,5},{5,6},{6,7},{11,8},{8,9},{9,10... | collective-permute-start | bytes 786440 | tf_op jit(solution)/shard_map/while/body/eval_jaxpr/ppermute | solution.py:28
  99.9 5.8 %collective-permute-start = (bf16[2,65536]{1,0:T(2,128)(2,1)S(1)}, bf16[2,65536]{1,0:T(2,128)(2,1)S(1)}, u32[]{:S(2)}, u32[]{:S(2)}) collective-permute-start(bf16[2,65536]{1,0:T(2,128)(2,1)S(1)} %get-tuple-element.244), channel_id=1, source_target_pairs={{3,0},{0,1},{1,2},{2,3},{7,4},{4,5},{5,6},{6,7},{11,8},{8,9},{9,10... | collective-permute-start | bytes 786440 | tf_op jit(solution)/shard_map/while/body/eval_jaxpr/ppermute | solution.py:28
  107.0 5.8 %collective-permute-start = (bf16[2,65536]{1,0:T(2,128)(2,1)S(1)}, bf16[2,65536]{1,0:T(2,128)(2,1)S(1)}, u32[]{:S(2)}, u32[]{:S(2)}) collective-permute-start(bf16[2,65536]{1,0:T(2,128)(2,1)S(1)} %get-tuple-element.244), channel_id=1, source_target_pairs={{3,0},{0,1},{1,2},{2,3},{7,4},{4,5},{5,6},{6,7},{11,8},{8,9},{9,10... | collective-permute-start | bytes 786440 | tf_op jit(solution)/shard_map/while/body/eval_jaxpr/ppermute | solution.py:28
Sparse Core Ops, SparseCore 0:
  55.1 35.3 all-reduce.1
where the time goes:
time: 151 us
  waiting for transfers between devices  70.7 us (47%)
  blocking collectives  26.4 us (17%)
  between operations  14.3 us (9%)
  starting transfers between devices  12.2 us (8%)
  other arithmetic  11.2 us (7%)
  matrix products  9.16 us (6%)
  local copies, waits for them, and re-layouts  7.04 us (5%)
    psum x1, waiting for transfers between devices, local(): lax.psum(member_sum.astype(jnp.bfloat16), 'member').astype(jnp.float32)  35.5 us
    psum x1, blocking collectives, local(): summed = lax.psum(gram_tile, 'space')  21.3 us
    ppermute x3, waiting for transfers between devices, from_behind(): return lax.ppermute(block, axis, route)  17.3 us
    ppermute x2, waiting for transfers between devices, extended_2(): lax.ppermute(lax.slice_in_dim(block, block.shape[dim] - width, None, axis...  12 us
    ppermute x2, starting transfers between devices, extended_2(): lax.ppermute(lax.slice_in_dim(block, block.shape[dim] - width, None, axis...  9.26 us
    dot_general x1, matrix products, local(): jnp.dot(pattern_pick, inflow_table.reshape(patterns, plane_rows * plane_c...  5.97 us
    ppermute x2, waiting for transfers between devices, extended_2(): lax.ppermute(lax.slice_in_dim(block, 0, width, axis=dim), axis, backward)  5.88 us
    all_gather x1, blocking collectives, local(): gram_full = lax.all_gather(summed, 'member', axis=0, tiled=True)  5.06 us
  transfers between devices with their start and end apart: 8, of which 7 were waited for; matrix products, arithmetic and copies ran while one was open for 1% of the time, Pallas kernels for 0%

commit v1 on v0

--- a/solution.py
+++ b/solution.py
@@ -7,6 +7,14 @@
 kappa_rate = 0.05
 shrink_weight = 0.1
 contract_dims = (((1,), (1,)), ((), ()))
+
+
+def added_up(block, axis):
+    size, total = (lax.axis_size(axis), block)
+    for far in [1 << k for k in range(size.bit_length() - 1)]:
+        swap = [(i, i ^ far) for i in range(size)]
+        total = total + lax.ppermute(total, axis, swap)
+    return total
 
 
 def extended_2(block, sides, width):
@@ -100,7 +108,7 @@
 
     gram_tile, panel_held = lax.fori_loop(1, groups, turn, (gram_tile, anomaly))
     gram_tile = gram_tile / cells_all
-    summed = lax.psum(gram_tile, "space")
+    summed = added_up(gram_tile, "space")
     gram_full = lax.all_gather(summed, "member", axis=0, tiled=True)
     r_factor = jnp.linalg.cholesky(
         gram_full + shrink_weight * jnp.eye(all_members, dtype=jnp.float32)

time: 151 us -> 141 us (0.934)
  blocking collectives: 26.4 us -> 5.06 us
  starting transfers between devices: 12.2 us -> 17.7 us
  waiting for transfers between devices: 70.7 us -> 76.1 us
    psum x1 -> x0, blocking collectives: 21.3 us -> none  [local(): summed = lax.psum(gram_tile, 'space')]
    ppermute x0 -> x3, starting transfers between devices: none -> 5.43 us  [added_up(): total = total + lax.ppermute(total, axis, swap)]
    ppermute x0 -> x3, waiting for transfers between devices: none -> 5.4 us  [added_up(): total = total + lax.ppermute(total, axis, swap)]
  transfers between devices with their start and end apart: 8 -> 11, of which waited for: 7 -> 10; matrix products, arithmetic and copies ran while one was open for 1% -> 1% of each run, Pallas kernels for 0% -> 0%
where the time goes in v1:
time: 141 us
  waiting for transfers between devices  76.1 us (54%)
  starting transfers between devices  17.7 us (13%)
  between operations  14.3 us (10%)
  other arithmetic  11.1 us (8%)
  matrix products  9.16 us (6%)
  local copies, waits for them, and re-layouts  7.04 us (5%)
  blocking collectives  5.06 us (4%)
    psum x1, waiting for transfers between devices, local(): lax.psum(member_sum.astype(jnp.bfloat16), 'member').astype(jnp.float32)  35.5 us
    ppermute x3, waiting for transfers between devices, from_behind(): return lax.ppermute(block, axis, route)  17.3 us
    ppermute x2, waiting for transfers between devices, extended_2(): lax.ppermute(lax.slice_in_dim(block, block.shape[dim] - width, None, axis...  12 us
    ppermute x2, starting transfers between devices, extended_2(): lax.ppermute(lax.slice_in_dim(block, block.shape[dim] - width, None, axis...  9.26 us
    dot_general x1, matrix products, local(): jnp.dot(pattern_pick, inflow_table.reshape(patterns, plane_rows * plane_c...  5.97 us
    ppermute x2, waiting for transfers between devices, extended_2(): lax.ppermute(lax.slice_in_dim(block, 0, width, axis=dim), axis, backward)  5.88 us
    ppermute x3, starting transfers between devices, added_up(): total = total + lax.ppermute(total, axis, swap)  5.43 us
    ppermute x3, waiting for transfers between devices, added_up(): total = total + lax.ppermute(total, axis, swap)  5.4 us
  transfers between devices with their start and end apart: 11, of which 10 were waited for; matrix products, arithmetic and copies ran while one was open for 1% of the time, Pallas kernels for 0%

profile of v1, /device:TPU:0, one launch (start us, length us, event | category | flops | bytes accessed | tf_op | source)
XLA Modules:
  0.0 140.6 jit_solution(3690197124955204420)
XLA Ops:
  7.2 1.4 %copy.24 = f32[2,2,128,256]{3,0,2,1:T(2,128)S(1)} copy(f32[2,2,128,256]{3,2,1,0:T(8,128)} %param.11) | data formatting | bytes 1048576 | tf_op args[0]
  8.9 4.9 %collective-permute-start.1 = (f32[2,1,128,256]{3,0,2,1:T(2,128)S(1)}, f32[2,1,128,256]{3,0,2,1:T(2,128)S(1)}, u32[]{:S(2)}, u32[]{:S(2)}) collective-permute-start(f32[2,1,128,256]{3,0,2,1:T(2,128)S(1)} %get-tuple-element.196), channel_id=1, source_target_pairs={{0,4},{4,8},{8,12},{12,16},{16,20},{20,24},{24,28},{1,5},{5,9},{9,... | collective-permute-start | bytes 786440 | tf_op jit(solution)/shard_map/ppermute | solution.py:25
  13.7 1.3 collective-permute-start.2
  16.0 8.9 %collective-permute-done.1 = f32[2,1,128,256]{3,0,2,1:T(2,128)S(1)} collective-permute-done((f32[2,1,128,256]{3,0,2,1:T(2,128)S(1)}, f32[2,1,128,256]{3,0,2,1:T(2,128)S(1)}, u32[]{:S(2)}, u32[]{:S(2)}) %collective-permute-start.1) | collective-permute-done | bytes 262176 | tf_op jit(solution)/shard_map/ppermute | solution.py:25
  25.4 6.0 %bitcast_dynamic-update-slice_fusion.1 = (f32[2,4,128,256]{3,0,2,1:T(2,128)S(1)}, f32[2,128,256]{2,0,1:T(2,128)S(1)}) fusion(f32[2,4,128,256]{3,0,2,1:T(2,128)S(1)} %pad_maximum_fusion, f32[2,1,128,256]{3,0,2,1:T(2,128)S(1)} %collective-permute-done.1, pred[]{:T(512)S(6)} %eq.25, s32[2]{0:T(128)S(1)} %copy-done.1, f32[4,8,128,256]{3,2,1,0:T(8,128)} %bitcast.52), kind=kOutput, calls=%fused_computation.27 | convolution fusion | flops 25231424 | bytes 4981249 | tf_op jit(solution)/shard_map/dot_general | solution.py:66
  32.7 1.9 %fusion.15 = f32[2,2,128,256]{3,0,2,1:T(2,128)S(1)} fusion(f32[2,2,128,1]{3,0,2,1:T(2,128)S(1)} %get-tuple-element.191, f32[2,2,128,255]{3,0,2,1:T(2,128)S(1)} %get-tuple-element.193, f32[2,2,128,255]{3,0,2,1:T(2,128)S(1)} %get-tuple-element.192, f32[2,2,128,1]{3,0,2,1:T(2,128)S(1)} %get-tuple-element.190, f32[2,2,1,256]{3,0,2,1:T(2,128)S(1)} %get-tuple-element.187, ...), kind=kLoop, calls=%fused_computation.23 | loop fusion | flops 2228224 | bytes 4718592 | tf_op jit(solution)/shard_map/mul | solution.py:49
  34.8 4.4 %collective-permute-start.3 = (f32[2,1,128,256]{3,0,2,1:T(2,128)S(1)}, f32[2,1,128,256]{3,0,2,1:T(2,128)S(1)}, u32[]{:S(2)}, u32[]{:S(2)}) collective-permute-start(f32[2,1,128,256]{3,0,2,1:T(2,128)S(1)} %get-tuple-element.194), channel_id=1, source_target_pairs={{0,4},{4,8},{8,12},{12,16},{16,20},{20,24},{24,28},{1,5},{5,9},{9,... | collective-permute-start | bytes 786440 | tf_op jit(solution)/shard_map/ppermute | solution.py:25
  39.2 1.5 %collective-permute-start.4 = (f32[2,1,128,256]{3,0,2,1:T(2,128)S(1)}, f32[2,1,128,256]{3,0,2,1:T(2,128)S(1)}, u32[]{:S(2)}, u32[]{:S(2)}) collective-permute-start(f32[2,1,128,256]{3,0,2,1:T(2,128)S(1)} %get-tuple-element.195), channel_id=1, source_target_pairs={{4,0},{8,4},{12,8},{16,12},{20,16},{24,20},{28,24},{5,1},{9,5},{13... | collective-permute-start | bytes 786440 | tf_op jit(solution)/shard_map/ppermute | solution.py:28
  40.7 3.2 %collective-permute-done.3 = f32[2,1,128,256]{3,0,2,1:T(2,128)S(1)} collective-permute-done((f32[2,1,128,256]{3,0,2,1:T(2,128)S(1)}, f32[2,1,128,256]{3,0,2,1:T(2,128)S(1)}, u32[]{:S(2)}, u32[]{:S(2)}) %collective-permute-start.3) | collective-permute-done | bytes 262176 | tf_op jit(solution)/shard_map/ppermute | solution.py:25
  43.9 5.9 %collective-permute-done.4 = f32[2,1,128,256]{3,0,2,1:T(2,128)S(1)} collective-permute-done((f32[2,1,128,256]{3,0,2,1:T(2,128)S(1)}, f32[2,1,128,256]{3,0,2,1:T(2,128)S(1)}, u32[]{:S(2)}, u32[]{:S(2)}) %collective-permute-start.4) | collective-permute-done | bytes 262176 | tf_op jit(solution)/shard_map/ppermute | solution.py:28
  51.8 3.2 %fusion.23 = (bf16[2,128,256]{2,1,0:T(8,128)(2,1)}, f32[2,2,128,256]{3,0,2,1:T(2,128)S(1)}) fusion(f32[2,2,128,1]{3,0,2,1:T(2,128)S(1)} %get-tuple-element.183, f32[2,2,128,255]{3,0,2,1:T(2,128)S(1)} %get-tuple-element.185, f32[2,2,128,255]{3,0,2,1:T(2,128)S(1)} %get-tuple-element.184, f32[2,2,128,1]{3,0,2,1:T(2,128)S(1)} %get-tuple-element.182, ...), kind=kLoop, calls=%fused_computation.46 | loop fusion | flops 2293760 | bytes 4849664 | tf_op jit(solution)/shard_map/reduce_sum | solution.py:80
  55.0 35.5 %all-reduce.2.cloned.1.call-done = bf16[2,128,256]{2,1,0:T(8,128)(2,1)} async-done(((bf16[2,128,256]{2,1,0:T(8,128)(2,1)}), bf16[2,128,256]{2,1,0:T(8,128)(2,1)}) %all-reduce.2.cloned.1.call-update) | async-done | bytes 131088 | tf_op jit(solution)/shard_map/psum | solution.py:82
  92.9 21.1 %while.19 = (s32[]{:T(128)}, f32[2,8]{1,0:T(2,128)S(1)}, bf16[2,65536]{1,0:T(2,128)(2,1)S(1)}, bf16[2,65536]{1,0:T(2,128)(2,1)S(1)}, s32[]{:T(128)}, /*index=5*/...) while((s32[]{:T(128)}, f32[2,8]{1,0:T(2,128)S(1)}, ...), condition=%wide.region_3.4_spmd, body=%wide.region_2.3_spmd.sunk | while | flops 524306 | bytes 2097520 | solution.py:109
  93.0 5.8 %collective-permute-done = bf16[2,65536]{1,0:T(2,128)(2,1)S(1)} collective-permute-done((bf16[2,65536]{1,0:T(2,128)(2,1)S(1)}, bf16[2,65536]{1,0:T(2,128)(2,1)S(1)}, u32[]{:S(2)}, u32[]{:S(2)}) %collective-permute-start) | collective-permute-done | bytes 262176 | tf_op jit(solution)/shard_map/while/body/eval_jaxpr/ppermute | solution.py:36
  100.0 5.8 %collective-permute-done = bf16[2,65536]{1,0:T(2,128)(2,1)S(1)} collective-permute-done((bf16[2,65536]{1,0:T(2,128)(2,1)S(1)}, bf16[2,65536]{1,0:T(2,128)(2,1)S(1)}, u32[]{:S(2)}, u32[]{:S(2)}) %collective-permute-start) | collective-permute-done | bytes 262176 | tf_op jit(solution)/shard_map/while/body/eval_jaxpr/ppermute | solution.py:36
  107.1 5.8 %collective-permute-done = bf16[2,65536]{1,0:T(2,128)(2,1)S(1)} collective-permute-done((bf16[2,65536]{1,0:T(2,128)(2,1)S(1)}, bf16[2,65536]{1,0:T(2,128)(2,1)S(1)}, u32[]{:S(2)}, u32[]{:S(2)}) %collective-permute-start) | collective-permute-done | bytes 262176 | tf_op jit(solution)/shard_map/while/body/eval_jaxpr/ppermute | solution.py:36
  114.0 1.5 %collective-permute-start.5 = (f32[2,8]{1,0:T(2,128)S(1)}, f32[2,8]{1,0:T(2,128)S(1)}, u32[]{:S(2)}, u32[]{:S(2)}) collective-permute-start(f32[2,8]{1,0:T(2,128)S(1)} %broadcast_multiply_fusion), channel_id=1, source_target_pairs={{0,4},{4,0},{8,12},{12,8},{16,20},{20,16},{24,28},{28,24},{1,5},{5... | collective-permute-start | bytes 200 | tf_op jit(solution)/shard_map/ppermute | solution.py:16
  115.5 2.1 %collective-permute-done.5 = f32[2,8]{1,0:T(2,128)S(1)} collective-permute-done((f32[2,8]{1,0:T(2,128)S(1)}, f32[2,8]{1,0:T(2,128)S(1)}, u32[]{:S(2)}, u32[]{:S(2)}) %collective-permute-start.5) | collective-permute-done | bytes 96 | tf_op jit(solution)/shard_map/ppermute | solution.py:16
  117.6 1.5 %collective-permute-start.6 = (f32[2,8]{1,0:T(2,128)S(1)}, f32[2,8]{1,0:T(2,128)S(1)}, u32[]{:S(2)}, u32[]{:S(2)}) collective-permute-start(f32[2,8]{1,0:T(2,128)S(1)} %fusion.22), channel_id=1, source_target_pairs={{0,8},{4,12},{8,0},{12,4},{16,24},{20,28},{24,16},{28,20},{1,9},{5... | collective-permute-start | bytes 200 | tf_op jit(solution)/shard_map/ppermute | solution.py:16
  119.1 2.1 %collective-permute-done.6 = f32[2,8]{1,0:T(2,128)S(1)} collective-permute-done((f32[2,8]{1,0:T(2,128)S(1)}, f32[2,8]{1,0:T(2,128)S(1)}, u32[]{:S(2)}, u32[]{:S(2)}) %collective-permute-start.6) | collective-permute-done | bytes 96 | tf_op jit(solution)/shard_map/ppermute | solution.py:16
  121.2 2.4 %collective-permute-start.7 = (f32[2,8]{1,0:T(2,128)S(1)}, f32[2,8]{1,0:T(2,128)S(1)}, u32[]{:S(2)}, u32[]{:S(2)}) collective-permute-start(f32[2,8]{1,0:T(2,128)S(1)} %add.129), channel_id=1, source_target_pairs={{0,16},{4,20},{8,24},{12,28},{16,0},{20,4},{24,8},{28,12},{1,17},{... | collective-permute-start | bytes 200 | tf_op jit(solution)/shard_map/ppermute | solution.py:16
  124.5 1.2 collective-permute-done.7
  125.7 5.1 %all-gather = f32[4,2,8]{2,1,0:T(2,128)S(1)} all-gather(f32[1,2,8]{2,1,0:T(2,128)S(1)} %add_bitcast_fusion), channel_id=1, replica_groups=mesh['space'=8,'member'=4] {'member'}, dimensions={0}, use_global_device_ids=true | all-gather | bytes 320 | tf_op jit(solution)/shard_map/all_gather | solution.py:112
  132.5 1.2 select_bitcast_fusion
  (52 shorter events, 13.8 us)
Async XLA Ops:
  7.2 18.2 %copy-start.1 = (s32[2]{0:T(128)S(1)}, s32[2]{0:T(128)}, u32[]{:S(2)}) copy-start(s32[2]{0:T(128)} %param.15) | copy-start | bytes 28
  7.2 83.3 %all-reduce.2.cloned.1.call-start = ((), (), s32[]{:S(2)}) async-start(), calls=%async_computation | async-start | bytes 262144 | tf_op jit(solution)/shard_map/psum | solution.py:82
  8.9 16.0 %collective-permute-start.1 = (f32[2,1,128,256]{3,0,2,1:T(2,128)S(1)}, f32[2,1,128,256]{3,0,2,1:T(2,128)S(1)}, u32[]{:S(2)}, u32[]{:S(2)}) collective-permute-start(f32[2,1,128,256]{3,0,2,1:T(2,128)S(1)} %get-tuple-element.196), channel_id=1, source_target_pairs={{0,4},{4,8},{8,12},{12,16},{16,20},{20,24},{24,28},{1,5},{5,9},{9,... | collective-permute-start | bytes 786440 | tf_op jit(solution)/shard_map/ppermute | solution.py:25
  13.7 11.2 %collective-permute-start.2 = (f32[2,1,128,256]{3,0,2,1:T(2,128)S(1)}, f32[2,1,128,256]{3,0,2,1:T(2,128)S(1)}, u32[]{:S(2)}, u32[]{:S(2)}) collective-permute-start(f32[2,1,128,256]{3,0,2,1:T(2,128)S(1)} %get-tuple-element.197), channel_id=1, source_target_pairs={{4,0},{8,4},{12,8},{16,12},{20,16},{24,20},{28,24},{5,1},{9,5},{13... | collective-permute-start | bytes 786440 | tf_op jit(solution)/shard_map/ppermute | solution.py:28
  25.4 7.3 %copy-start = (f32[2,128,256]{2,1,0:T(8,128)S(1)}, f32[2,128,256]{2,1,0:T(8,128)}, u32[]{:S(2)}) copy-start(f32[2,128,256]{2,1,0:T(8,128)} %param.12) | copy-start | bytes 786436
  34.8 9.1 %collective-permute-start.3 = (f32[2,1,128,256]{3,0,2,1:T(2,128)S(1)}, f32[2,1,128,256]{3,0,2,1:T(2,128)S(1)}, u32[]{:S(2)}, u32[]{:S(2)}) collective-permute-start(f32[2,1,128,256]{3,0,2,1:T(2,128)S(1)} %get-tuple-element.194), channel_id=1, source_target_pairs={{0,4},{4,8},{8,12},{12,16},{16,20},{20,24},{24,28},{1,5},{5,9},{9,... | collective-permute-start | bytes 786440 | tf_op jit(solution)/shard_map/ppermute | solution.py:25
  39.2 10.5 %collective-permute-start.4 = (f32[2,1,128,256]{3,0,2,1:T(2,128)S(1)}, f32[2,1,128,256]{3,0,2,1:T(2,128)S(1)}, u32[]{:S(2)}, u32[]{:S(2)}) collective-permute-start(f32[2,1,128,256]{3,0,2,1:T(2,128)S(1)} %get-tuple-element.195), channel_id=1, source_target_pairs={{4,0},{8,4},{12,8},{16,12},{20,16},{24,20},{28,24},{5,1},{9,5},{13... | collective-permute-start | bytes 786440 | tf_op jit(solution)/shard_map/ppermute | solution.py:28
  92.9 5.8 %collective-permute-start = (bf16[2,65536]{1,0:T(2,128)(2,1)S(1)}, bf16[2,65536]{1,0:T(2,128)(2,1)S(1)}, u32[]{:S(2)}, u32[]{:S(2)}) collective-permute-start(bf16[2,65536]{1,0:T(2,128)(2,1)S(1)} %get-tuple-element.244), channel_id=1, source_target_pairs={{3,0},{0,1},{1,2},{2,3},{7,4},{4,5},{5,6},{6,7},{11,8},{8,9},{9,10... | collective-permute-start | bytes 786440 | tf_op jit(solution)/shard_map/while/body/eval_jaxpr/ppermute | solution.py:36
  99.9 5.8 %collective-permute-start = (bf16[2,65536]{1,0:T(2,128)(2,1)S(1)}, bf16[2,65536]{1,0:T(2,128)(2,1)S(1)}, u32[]{:S(2)}, u32[]{:S(2)}) collective-permute-start(bf16[2,65536]{1,0:T(2,128)(2,1)S(1)} %get-tuple-element.244), channel_id=1, source_target_pairs={{3,0},{0,1},{1,2},{2,3},{7,4},{4,5},{5,6},{6,7},{11,8},{8,9},{9,10... | collective-permute-start | bytes 786440 | tf_op jit(solution)/shard_map/while/body/eval_jaxpr/ppermute | solution.py:36
  107.0 5.8 %collective-permute-start = (bf16[2,65536]{1,0:T(2,128)(2,1)S(1)}, bf16[2,65536]{1,0:T(2,128)(2,1)S(1)}, u32[]{:S(2)}, u32[]{:S(2)}) collective-permute-start(bf16[2,65536]{1,0:T(2,128)(2,1)S(1)} %get-tuple-element.244), channel_id=1, source_target_pairs={{3,0},{0,1},{1,2},{2,3},{7,4},{4,5},{5,6},{6,7},{11,8},{8,9},{9,10... | collective-permute-start | bytes 786440 | tf_op jit(solution)/shard_map/while/body/eval_jaxpr/ppermute | solution.py:36
  114.0 3.6 %collective-permute-start.5 = (f32[2,8]{1,0:T(2,128)S(1)}, f32[2,8]{1,0:T(2,128)S(1)}, u32[]{:S(2)}, u32[]{:S(2)}) collective-permute-start(f32[2,8]{1,0:T(2,128)S(1)} %broadcast_multiply_fusion), channel_id=1, source_target_pairs={{0,4},{4,0},{8,12},{12,8},{16,20},{20,16},{24,28},{28,24},{1,5},{5... | collective-permute-start | bytes 200 | tf_op jit(solution)/shard_map/ppermute | solution.py:16
  117.6 3.6 %collective-permute-start.6 = (f32[2,8]{1,0:T(2,128)S(1)}, f32[2,8]{1,0:T(2,128)S(1)}, u32[]{:S(2)}, u32[]{:S(2)}) collective-permute-start(f32[2,8]{1,0:T(2,128)S(1)} %fusion.22), channel_id=1, source_target_pairs={{0,8},{4,12},{8,0},{12,4},{16,24},{20,28},{24,16},{28,20},{1,9},{5... | collective-permute-start | bytes 200 | tf_op jit(solution)/shard_map/ppermute | solution.py:16
  121.2 4.5 %collective-permute-start.7 = (f32[2,8]{1,0:T(2,128)S(1)}, f32[2,8]{1,0:T(2,128)S(1)}, u32[]{:S(2)}, u32[]{:S(2)}) collective-permute-start(f32[2,8]{1,0:T(2,128)S(1)} %add.129), channel_id=1, source_target_pairs={{0,16},{4,20},{8,24},{12,28},{16,0},{20,4},{24,8},{28,12},{1,17},{... | collective-permute-start | bytes 200 | tf_op jit(solution)/shard_map/ppermute | solution.py:16
Sparse Core Ops, SparseCore 0:
  55.1 35.3 all-reduce.1
